TPU v7x, 32 devices: a whole 2x2x4 slice. The times are simulated.
32 devices in a mesh: groups: 2 (over y), loop: 4 (over z), rep: 4 (over x, core).
Axes of the slice: x: 2, y: 2, z: 4, core: 2. Of those that a mesh axis runs over, the one named last changes fastest.
Arguments:
- features: bfloat16 [8192, 512], P(('groups', 'loop', 'rep')), parts along dimension 0, may hold values from -6 to 6
- weight: bfloat16 [512, 512], replicated, may hold values from -0.25 to 0.25
- block_row: int32 [8, 4, 4, 6], P(('groups', 'loop'), 'rep'), parts along dimension 0, may hold values from 0 to 7
- edge_row: int32 [8, 4, 4, 6, 64], P(('groups', 'loop'), 'rep'), parts along dimension 0, may hold values from 0 to 127
- edge_col: int32 [8, 4, 4, 6, 64], P(('groups', 'loop'), 'rep'), parts along dimension 0, may hold values from 0 to 255
- edge_count: int32 [8, 4, 4, 6, 64], P(('groups', 'loop'), 'rep'), parts along dimension 0, may hold values from 1 to 3
Outputs:
- activated: bfloat16 [8192, 512], P(('groups', 'loop', 'rep')), parts along dimension 0
There are 2 independent parts, one for each index of `groups`. A program takes and returns all parts, laid end to end along the dimension named above; an argument that names none is the same for every part. Nothing has to cross between parts.
All inputs are finite; a program needn't handle non-finite values.
Results may differ from a plain program's by a relative error of at most 0.0085.
Values may be sent and summed in bfloat16 or wider, within the bound.
A program may use at most 64 MiB of HBM per device.

v0:
```python
import jax
import jax.numpy as jnp
from jax import lax
from jax.sharding import PartitionSpec as P

BLOCK = 128


def passed_along(value, axis, steps):
    count = lax.axis_size(axis)
    pairs = [(source, (source + steps) % count) for source in range(count)]
    return lax.ppermute(value, axis, pairs)


def body(features, weight, block_row, edge_row, edge_col, edge_count):
    loop_count = lax.axis_size("loop")
    rep_count = lax.axis_size("rep")
    my_loop = lax.axis_index("loop")
    own_rows, feat_width = features.shape
    slot_count = edge_row.shape[3]
    edge_per = edge_row.shape[4]
    per_source = slot_count * edge_per
    loop_rows = rep_count * own_rows
    block_count = loop_rows // BLOCK
    row_blocks = block_row.reshape(loop_count, slot_count)
    edge_rows = edge_row.reshape(loop_count, slot_count, edge_per)
    edge_cols = edge_col.reshape(loop_count, per_source)
    edge_weights = edge_count.reshape(loop_count, slot_count, edge_per)
    targets = (row_blocks[:, :, None] * BLOCK + edge_rows).reshape(-1)
    degree = jax.ops.segment_sum(
        edge_weights.reshape(-1).astype(jnp.float32), targets, num_segments=loop_rows
    )
    block_pos = jnp.arange(BLOCK, dtype=jnp.int32)

    def add_blocks(aggregate, rows_now, weights_now, blocks_now, picked):
        onehot = jnp.where(
            block_pos[None, :, None] == rows_now[:, None, :],
            weights_now[:, None, :].astype(jnp.float32),
            0.0,
        ).astype(jnp.bfloat16)
        blocks = jnp.einsum("sbe,sef->sbf", onehot, picked, preferred_element_type=jnp.float32)
        return aggregate.at[blocks_now].add(blocks)

    aggregate = jnp.zeros((block_count, BLOCK, feat_width), jnp.float32)

    def absorb(aggregate, visiting, anchor):
        rows_now = lax.dynamic_index_in_dim(edge_rows, anchor, 0, keepdims=False)
        weights_now = lax.dynamic_index_in_dim(edge_weights, anchor, 0, keepdims=False)
        cols_now = lax.dynamic_index_in_dim(edge_cols, anchor, 0, keepdims=False)
        blocks_now = lax.dynamic_index_in_dim(row_blocks, anchor, 0, keepdims=False)
        picked = jnp.take(visiting, cols_now, axis=0).reshape(slot_count, edge_per, feat_width)
        return add_blocks(aggregate, rows_now, weights_now, blocks_now, picked)

    def advance(turn, state_now):
        aggregate, visiting = state_now
        aggregate = absorb(aggregate, visiting, (my_loop - turn) % loop_count)
        visiting = passed_along(visiting, "loop", 1)
        return (aggregate, visiting)

    aggregate, visiting = lax.fori_loop(0, loop_count - 1, advance, (aggregate, features))
    aggregate = absorb(aggregate, visiting, (my_loop - (loop_count - 1)) % loop_count)
    aggregate = aggregate.reshape(loop_rows, feat_width)
    shares, degree_share = (
        lax.psum_scatter(
            aggregate.astype(jnp.bfloat16), "rep", scatter_dimension=0, tiled=True
        ).astype(jnp.float32),
        lax.psum_scatter(
            degree.astype(jnp.bfloat16), "rep", scatter_dimension=0, tiled=True
        ).astype(jnp.float32),
    )
    normalized = ((shares + features.astype(jnp.float32)) / (degree_share[:, None] + 1.0)).astype(
        jnp.bfloat16
    )
    product = jnp.dot(normalized, weight, preferred_element_type=jnp.float32)
    return jnp.maximum(product, 0.0).astype(jnp.bfloat16)


def solution(mesh):
    return jax.shard_map(
        body,
        mesh=mesh,
        in_specs=(
            P(("groups", "loop", "rep"), None),
            P(),
            P(("groups", "loop"), "rep", None, None),
            P(("groups", "loop"), "rep", None, None, None),
            P(("groups", "loop"), "rep", None, None, None),
            P(("groups", "loop"), "rep", None, None, None),
        ),
        out_specs=P(("groups", "loop", "rep"), None),
        check_vma=False,
    )
```

profile of v0, /device:TPU:0, one launch (start us, length us, event | category | flops | bytes accessed | tf_op | source)
XLA Modules:
  0.0 81.4 jit_solution(6264598117551271634)
XLA Ops:
  6.6 0.8 copy.19
  7.5 0.7 fusion.18
  8.2 0.7 fusion.20
  8.9 1.6 %broadcast_in_dim.73 = f32[8,128,512]{2,1,0:T(8,128)} broadcast(f32[]{:T(128)} %constant.121.clone.1), dimensions={} | broadcast | bytes 2097156 | tf_op jit(solution)/shard_map/broadcast_in_dim | solution.py:44
  10.6 29.2 %while.18 = (s32[]{:T(128)}, f32[8,128,512]{2,1,0:T(8,128)}, bf16[256,512]{1,0:T(8,128)(2,1)S(1)}, s32[]{:T(128)}, s32[4,6]{1,0:T(4,128)S(1)}, /*index=5*/s32[4,...) while((s32[]{:T(128)}, f32[8,128,512]{2,1,0:T(8,128)}, ...), condition=%wide.region_2.4_spmd.clone, body=%wide.region_0.3_spmd.clone.sunk | while | flops 51024672 | bytes 9854092 | solution.py:60
  10.6 3.1 %collective-permute-start = (bf16[256,512]{1,0:T(8,128)(2,1)S(1)}, bf16[256,512]{1,0:T(8,128)(2,1)S(1)}, u32[]{:S(2)}, u32[]{:S(2)}) collective-permute-start(bf16[256,512]{1,0:T(8,128)(2,1)S(1)} %copy.34), channel_id=1, source_target_pairs={{0,4},{4,8},{8,12},{12,0},{1,5},{5,9},{9,13},{13,1},{2,6},{6,10},{... | collective-permute-start | bytes 786440 | tf_op jit(solution)/shard_map/while/body/eval_jaxpr/ppermute | solution.py:12
  13.7 2.1 %gather_fusion = bf16[384,512]{1,0:T(8,128)(2,1)S(1)} fusion(bf16[256,512]{1,0:T(8,128)(2,1)S(1)} %copy.34, s32[1024]{0:T(1024)S(1)} %pad_clamp_fusion.3), kind=kCustom, calls=%fused_computation.clone.clone.1 | custom fusion | bytes 787968 | tf_op jit(solution)/shard_map/while/body/eval_jaxpr/jit(_take)/gather | solution.py:51
  15.8 0.1 broadcast_select_fusion.3
  15.9 0.6 fusion.30
  16.6 3.9 %scatter_fusion = f32[8,128,512]{2,1,0:T(8,128)} fusion(f32[8,128,512]{2,1,0:T(8,128)} %get-tuple-element.338, s32[6]{0:T(128)S(1)} %fusion.29, f32[6,128,512]{2,1,0:T(8,128)S(1)} %fusion.30), kind=kCustom, calls=%fused_computation.2.clone.clone.1 | custom fusion | flops 393216 | bytes 4718616 | tf_op jit(solution)/shard_map/while/body/eval_jaxpr/scatter-add | solution.py:42
  20.5 1.5 %collective-permute-done = bf16[256,512]{1,0:T(8,128)(2,1)S(1)} collective-permute-done((bf16[256,512]{1,0:T(8,128)(2,1)S(1)}, bf16[256,512]{1,0:T(8,128)(2,1)S(1)}, u32[]{:S(2)}, u32[]{:S(2)}) %collective-permute-start) | collective-permute-done | bytes 262176 | tf_op jit(solution)/shard_map/while/body/eval_jaxpr/ppermute | solution.py:12
  22.0 0.1 collective-permute-start
  22.2 2.1 %gather_fusion = bf16[384,512]{1,0:T(8,128)(2,1)S(1)} fusion(bf16[256,512]{1,0:T(8,128)(2,1)S(1)} %copy.34, s32[1024]{0:T(1024)S(1)} %pad_clamp_fusion.3), kind=kCustom, calls=%fused_computation.clone.clone.1 | custom fusion | bytes 787968 | tf_op jit(solution)/shard_map/while/body/eval_jaxpr/jit(_take)/gather | solution.py:51
  24.3 0.1 broadcast_select_fusion.3
  24.4 0.6 fusion.30
  25.0 3.8 %scatter_fusion = f32[8,128,512]{2,1,0:T(8,128)} fusion(f32[8,128,512]{2,1,0:T(8,128)} %get-tuple-element.338, s32[6]{0:T(128)S(1)} %fusion.29, f32[6,128,512]{2,1,0:T(8,128)S(1)} %fusion.30), kind=kCustom, calls=%fused_computation.2.clone.clone.1 | custom fusion | flops 393216 | bytes 4718616 | tf_op jit(solution)/shard_map/while/body/eval_jaxpr/scatter-add | solution.py:42
  28.9 2.5 %collective-permute-done = bf16[256,512]{1,0:T(8,128)(2,1)S(1)} collective-permute-done((bf16[256,512]{1,0:T(8,128)(2,1)S(1)}, bf16[256,512]{1,0:T(8,128)(2,1)S(1)}, u32[]{:S(2)}, u32[]{:S(2)}) %collective-permute-start) | collective-permute-done | bytes 262176 | tf_op jit(solution)/shard_map/while/body/eval_jaxpr/ppermute | solution.py:12
  31.5 2.1 %gather_fusion = bf16[384,512]{1,0:T(8,128)(2,1)S(1)} fusion(bf16[256,512]{1,0:T(8,128)(2,1)S(1)} %copy.34, s32[1024]{0:T(1024)S(1)} %pad_clamp_fusion.3), kind=kCustom, calls=%fused_computation.clone.clone.1 | custom fusion | bytes 787968 | tf_op jit(solution)/shard_map/while/body/eval_jaxpr/jit(_take)/gather | solution.py:51
  33.6 0.1 broadcast_select_fusion.3
  33.8 0.6 fusion.30
  34.4 3.9 %scatter_fusion = f32[8,128,512]{2,1,0:T(8,128)} fusion(f32[8,128,512]{2,1,0:T(8,128)} %get-tuple-element.338, s32[6]{0:T(128)S(1)} %fusion.29, f32[6,128,512]{2,1,0:T(8,128)S(1)} %fusion.30), kind=kCustom, calls=%fused_computation.2.clone.clone.1 | custom fusion | flops 393216 | bytes 4718616 | tf_op jit(solution)/shard_map/while/body/eval_jaxpr/scatter-add | solution.py:42
  38.2 1.6 %collective-permute-done = bf16[256,512]{1,0:T(8,128)(2,1)S(1)} collective-permute-done((bf16[256,512]{1,0:T(8,128)(2,1)S(1)}, bf16[256,512]{1,0:T(8,128)(2,1)S(1)}, u32[]{:S(2)}, u32[]{:S(2)}) %collective-permute-start) | collective-permute-done | bytes 262176 | tf_op jit(solution)/shard_map/while/body/eval_jaxpr/ppermute | solution.py:12
  39.8 2.1 %gather_fusion.1 = bf16[384,512]{1,0:T(8,128)(2,1)S(1)} fusion(bf16[256,512]{1,0:T(8,128)(2,1)S(1)} %get-tuple-element.229, s32[1024]{0:T(1024)S(1)} %pad_clamp_fusion.1), kind=kCustom, calls=%fused_computation.1.clone | custom fusion | bytes 787968 | tf_op jit(solution)/shard_map/jit(_take)/gather | solution.py:51
  41.9 0.1 broadcast_select_fusion.1
  42.0 1.8 %fusion.11 = f32[6,128,512]{2,1,0:T(8,128)} fusion(bf16[6,64,512]{2,1,0:T(8,128)(2,1)S(1)} %bitcast.49, bf16[6,64]{1,0:T(8,128)(2,1)S(1)} %convert_bitcast_fusion.1, s32[6,64]{1,0:T(8,128)S(1)} %dynamic-slice_bitcast_fusion.1), kind=kOutput, calls=%fused_computation.31 | convolution fusion | flops 50429952 | bytes 1968384 | tf_op jit(solution)/shard_map/sbe,sef->sbf/dot_general | solution.py:41
  43.8 2.8 %scatter_fusion.1 = f32[8,128,512]{2,1,0:T(8,128)S(1)} fusion(f32[8,128,512]{2,1,0:T(8,128)S(1)} %copy-done.1, s32[6]{0:T(128)S(1)} %fusion.18, f32[6,128,512]{2,1,0:T(8,128)} %fusion.11), kind=kCustom, calls=%fused_computation.3 | custom fusion | flops 393216 | bytes 4718616 | tf_op jit(solution)/shard_map/scatter-add | solution.py:42
  46.6 1.1 %convert_element_type.75 = bf16[8,128,512]{2,1,0:T(8,128)(2,1)} convert(f32[8,128,512]{2,1,0:T(8,128)S(1)} %scatter_fusion.1) | non-fusion elementwise | flops 524288 | bytes 3145728 | tf_op jit(solution)/shard_map/convert_element_type | solution.py:65
  48.2 11.1 %scatter_custom_fusion.2 = f32[1024]{0:T(1024)S(1)} fusion(s32[1536]{0:T(1024)S(1)} %add_reduce_fusion, f32[1536]{0:T(1024)S(1)} %reshape.204, f32[]{:T(128)} %constant.121.clone.1), kind=kCustom, calls=%fused_computation.41 | custom fusion | flops 1536 | bytes 4100 | tf_op jit(solution)/shard_map/scatter-add | solution.py:30
  59.3 0.6 dynamic-slice.3
  60.6 5.7 %all-reduce = bf16[1024]{0:T(1024)(128)(2,1)S(1)} all-reduce(bf16[1024]{0:T(1024)(128)(2,1)S(1)} %convert_element_type.81), channel_id=3, replica_groups=mesh['groups'=2,'loop'=4,'rep'=4] {'rep'}, use_global_device_ids=true, to_apply=%region_6.8.clone | all-reduce | flops 1024 | bytes 4096
  66.3 6.2 %reduce-scatter.2.cloned.1.call-done = bf16[256,512]{1,0:T(8,128)(2,1)} async-done(((bf16[1024,512]{1,0:T(8,128)(2,1)}), bf16[256,512]{1,0:T(8,128)(2,1)}) %reduce-scatter.2.cloned.1.call-update) | async-done | bytes 262160 | tf_op jit(solution)/shard_map/reduce_scatter | solution.py:64
  72.6 2.0 %fusion.9 = bf16[256,512]{1,0:T(8,128)(2,1)} fusion(bf16[512,512]{1,0:T(8,128)(2,1)S(1)} %copy-done, bf16[256,512]{1,0:T(8,128)(2,1)S(1)} %copy-done.2, bf16[256,512]{1,0:T(8,128)(2,1)} %reduce-scatter.2.cloned.1.call-done, f32[256]{0:T(256)S(1)} %convert_add_fusion), kind=kOutput, calls=%fused_computation.25 | convolution fusion | flops 135135232 | bytes 1311744 | tf_op jit(solution)/shard_map/dot_general | solution.py:74
  (55 shorter events, 0.9 us)
Async XLA Ops:
  6.5 66.0 %copy-start = (bf16[512,512]{1,0:T(8,128)(2,1)S(1)}, bf16[512,512]{1,0:T(8,128)(2,1)}, u32[]{:S(2)}) copy-start(bf16[512,512]{1,0:T(8,128)(2,1)} %param.11) | copy-start | bytes 1572868
  6.5 4.0 %copy-start.5 = (s32[1,1,4,6]{3,2,1,0:T(4,128)S(1)}, s32[1,1,4,6]{3,2,1,0:T(4,128)}, u32[]{:S(2)}) copy-start(s32[1,1,4,6]{3,2,1,0:T(4,128)} %param.12) | copy-start | bytes 292
  6.5 4.0 %copy-start.3 = (bf16[256,512]{1,0:T(8,128)(2,1)S(1)}, bf16[256,512]{1,0:T(8,128)(2,1)}, u32[]{:S(2)}) copy-start(bf16[256,512]{1,0:T(8,128)(2,1)} %param.10) | copy-start | bytes 786436
  6.5 66.0 %reduce-scatter.2.cloned.1.call-start = ((), (), s32[]{:S(2)}) async-start(), calls=%async_computation.1 | async-start | bytes 1310720 | tf_op jit(solution)/shard_map/reduce_scatter | solution.py:64
  10.6 11.4 %collective-permute-start = (bf16[256,512]{1,0:T(8,128)(2,1)S(1)}, bf16[256,512]{1,0:T(8,128)(2,1)S(1)}, u32[]{:S(2)}, u32[]{:S(2)}) collective-permute-start(bf16[256,512]{1,0:T(8,128)(2,1)S(1)} %copy.34), channel_id=1, source_target_pairs={{0,4},{4,8},{8,12},{12,0},{1,5},{5,9},{9,13},{13,1},{2,6},{6,10},{... | collective-permute-start | bytes 786440 | tf_op jit(solution)/shard_map/while/body/eval_jaxpr/ppermute | solution.py:12
  22.0 9.3 %collective-permute-start = (bf16[256,512]{1,0:T(8,128)(2,1)S(1)}, bf16[256,512]{1,0:T(8,128)(2,1)S(1)}, u32[]{:S(2)}, u32[]{:S(2)}) collective-permute-start(bf16[256,512]{1,0:T(8,128)(2,1)S(1)} %copy.34), channel_id=1, source_target_pairs={{0,4},{4,8},{8,12},{12,0},{1,5},{5,9},{9,13},{13,1},{2,6},{6,10},{... | collective-permute-start | bytes 786440 | tf_op jit(solution)/shard_map/while/body/eval_jaxpr/ppermute | solution.py:12
  31.4 8.4 %collective-permute-start = (bf16[256,512]{1,0:T(8,128)(2,1)S(1)}, bf16[256,512]{1,0:T(8,128)(2,1)S(1)}, u32[]{:S(2)}, u32[]{:S(2)}) collective-permute-start(bf16[256,512]{1,0:T(8,128)(2,1)S(1)} %copy.34), channel_id=1, source_target_pairs={{0,4},{4,8},{8,12},{12,0},{1,5},{5,9},{9,13},{13,1},{2,6},{6,10},{... | collective-permute-start | bytes 786440 | tf_op jit(solution)/shard_map/while/body/eval_jaxpr/ppermute | solution.py:12
  41.9 1.9 %copy-start.1 = (f32[8,128,512]{2,1,0:T(8,128)S(1)}, f32[8,128,512]{2,1,0:T(8,128)}, u32[]{:S(2)}) copy-start(f32[8,128,512]{2,1,0:T(8,128)} %get-tuple-element.228) | copy-start | bytes 6291460
  46.6 1.2 %copy-start.4 = (s32[1,1,4,6,64]{4,2,3,1,0:T(4,128)S(1)}, s32[1,1,4,6,64]{4,2,3,1,0:T(4,128)}, u32[]{:S(2)}) copy-start(s32[1,1,4,6,64]{4,2,3,1,0:T(4,128)} %param.15) | copy-start | bytes 18436
  46.6 12.7 %copy-start.6 = (u32[32]{0:T(128)S(1)}, u32[32]{0:T(128)}, u32[]{:S(2)}) copy-start(u32[32]{0:T(128)} %constant.136) | copy-start | bytes 388
  46.6 26.0 %copy-start.2 = (bf16[256,512]{1,0:T(8,128)(2,1)S(1)}, bf16[256,512]{1,0:T(8,128)(2,1)}, u32[]{:S(2)}) copy-start(bf16[256,512]{1,0:T(8,128)(2,1)} %param.10) | copy-start | bytes 786436
Sparse Core Ops, SparseCore 0:
  47.9 24.6 reduce-scatter.1
where the time goes:
time: 81.8 us; the launch traced here: 81.4 us
  other arithmetic  28.2 us (34%)
  between operations  14.2 us (17%)
  local copies, waits for them, and re-layouts  12.5 us (15%)
  waiting for transfers between devices  11.8 us (14%)
  blocking collectives  5.67 us (7%)
  matrix products  5.57 us (7%)
  starting transfers between devices  3.28 us (4%)
    scatter-add x4, other arithmetic, add_blocks(): return aggregate.at[blocks_now].add(blocks)  14.4 us
    scatter-add x1, other arithmetic, body(): jax.ops.segment_sum(edge_weights.reshape(-1).astype(jnp.float32), targets...  11.1 us
    gather x4, local copies, waits for them, and re-layouts, absorb(): jnp.take(visiting, cols_now, axis=0)  8.25 us
    reduce_scatter x1, waiting for transfers between devices, body(): lax.psum_scatter(aggregate.astype(jnp.bfloat16), 'rep', scatter_dimension...  6.25 us
    unnamed x1, blocking collectives  5.67 us
    ppermute x3, waiting for transfers between devices, passed_along(): return lax.ppermute(value, axis, pairs)  5.54 us
    dot_general x4, matrix products, add_blocks(): jnp.einsum('sbe,sef->sbf', onehot, picked, preferred_element_type=jnp.flo...  3.57 us
    ppermute x3, starting transfers between devices, passed_along(): return lax.ppermute(value, axis, pairs)  3.28 us
  transfers between devices with their start and end apart: 4, of which 4 were waited for; matrix products, arithmetic and copies ran while one was open for 40% of the time, Pallas kernels for 0%

commit v1 on v0

v1 whole, which is shorter than its diff:
```python
import functools

import jax
import jax.numpy as jnp
from jax import lax
from jax.experimental import pallas as pl
from jax.experimental.pallas import tpu as pltpu
from jax.sharding import PartitionSpec as P

BLOCK = 128
CHUNK = 128
MESH = pl.DeviceIdType.MESH
NT = (((1,), (1,)), ((), ()))


def repeat(count, step, most=4):
    if count <= most:
        for index in range(count):
            step(index)
    else:
        lax.fori_loop(0, count, lambda index, carry: (step(index), carry)[1], 0)


def kernel(
    loops, reps,
    feat_hbm, weight_hbm, brow_hbm, erow_hbm, ecol_hbm, ecnt_hbm,
    out_ref,
    gathered, adjacency, part_out, part_in, deg_out, deg_in, normal,
    weight_v, brow_s, erow_v, ecol_v, ecnt_v,
    local_sem, up_send, down_send, gather_recv, part_send, part_recv, deg_send, deg_recv,
):
    own, width = feat_hbm.shape
    chunks = width // CHUNK
    slots, edges = erow_v.shape[1:]
    z = lax.axis_index("loop")
    me = lax.axis_index("rep")
    has_up = z < loops - 1
    has_down = z > 0

    def rows(index):
        return pl.ds(pl.multiple_of(index * own, own), own)

    small = [
        pltpu.make_async_copy(brow_hbm, brow_s, local_sem.at[0]),
        pltpu.make_async_copy(erow_hbm, erow_v, local_sem.at[1]),
        pltpu.make_async_copy(ecol_hbm, ecol_v, local_sem.at[2]),
        pltpu.make_async_copy(ecnt_hbm, ecnt_v, local_sem.at[3]),
    ]
    weight_copy = pltpu.make_async_copy(weight_hbm, weight_v, local_sem.at[4])
    own_copy = [
        pltpu.make_async_copy(
            feat_hbm.at[:, pl.ds(c * CHUNK, CHUNK)], gathered.at[c, rows(z)], local_sem.at[5 + c]
        )
        for c in range(chunks)
    ]
    for copy in own_copy + small + [weight_copy]:
        copy.start()

    barrier = pltpu.get_barrier_semaphore()

    @pl.when(has_up)
    def _():
        pl.semaphore_signal(barrier, inc=1, device_id={"loop": z + 1}, device_id_type=MESH)

    @pl.when(has_down)
    def _():
        pl.semaphore_signal(barrier, inc=1, device_id={"loop": z - 1}, device_id_type=MESH)

    for k in range(1, reps):
        pl.semaphore_signal(
            barrier, inc=1, device_id={"rep": lax.rem(me + k, reps)}, device_id_type=MESH
        )
    pl.semaphore_wait(barrier, reps - 1 + has_up.astype(jnp.int32) + has_down.astype(jnp.int32))

    def shift(source, c, up):
        return pltpu.make_async_remote_copy(
            src_ref=gathered.at[c, rows(source)],
            dst_ref=gathered.at[c, rows(source)],
            send_sem=(up_send if up else down_send).at[source, c],
            recv_sem=gather_recv.at[source, c],
            device_id={"loop": z + 1 if up else z - 1},
            device_id_type=MESH,
        )

    for c in range(chunks):
        own_copy[c].wait()

        @pl.when(has_up)
        def _():
            shift(z, c, True).start()

        @pl.when(has_down)
        def _():
            shift(z, c, False).start()

    for copy in small:
        copy.wait()
    listed = slots * edges
    target_pos = lax.broadcasted_iota(jnp.int32, (own, listed), 0)
    source_pos = lax.broadcasted_iota(jnp.int32, (own, listed), 0)
    ones = jnp.ones((8, listed), jnp.bfloat16)

    def joined(ref, source, offset=None):
        pieces = []
        for s in range(slots):
            piece = ref[source, s : s + 1, :]
            if offset is not None:
                piece = piece + offset(s)
            pieces.append(piece)
        return jnp.concatenate(pieces, axis=1)

    deg_out[...] = jnp.zeros_like(deg_out)

    def build(source):
        target = joined(erow_v, source, lambda s: brow_s[source, s] * BLOCK)
        column = joined(ecol_v, source)
        count = joined(ecnt_v, source).astype(jnp.float32)
        pick = jnp.where(source_pos == column, 1.0, 0.0).astype(jnp.bfloat16)

        def build_rows(r):
            place = jnp.where(target_pos == target - r * own, count, 0.0).astype(jnp.bfloat16)
            block = lax.dot_general(place, pick, NT, preferred_element_type=jnp.float32)
            adjacency[rows(r), rows(source)] = block.astype(jnp.bfloat16)
            deg_out[r] += lax.dot_general(ones, place, NT, preferred_element_type=jnp.float32)

        repeat(reps, build_rows)

    repeat(loops, build)

    def deg_copy(r):
        return pltpu.make_async_remote_copy(
            src_ref=deg_out.at[r],
            dst_ref=deg_in.at[me],
            send_sem=deg_send.at[r],
            recv_sem=deg_recv.at[me],
            device_id={"rep": r},
            device_id_type=MESH,
        )

    def deg_arrival(r):
        return pltpu.make_async_remote_copy(
            src_ref=deg_out.at[r],
            dst_ref=deg_in.at[r],
            send_sem=deg_send.at[r],
            recv_sem=deg_recv.at[r],
            device_id={"rep": r},
            device_id_type=MESH,
        )

    deg_out[...] = deg_out[...].astype(jnp.bfloat16).astype(jnp.float32)
    deg_in[me] = deg_out[me]
    for k in range(1, reps):
        deg_copy(lax.rem(me + k, reps)).start()

    def gather(c):
        def hop(index):
            below = z - 1 - index
            above = z + 1 + index

            @pl.when(below >= 0)
            def _():
                copy = shift(below, c, True)
                copy.wait_recv()

                @pl.when(has_up)
                def _():
                    copy.start()

            @pl.when(above < loops)
            def _():
                copy = shift(above, c, False)
                copy.wait_recv()

                @pl.when(has_down)
                def _():
                    copy.start()

        repeat(loops - 1, hop)

    seg = min(loops, 4) * own
    segs = loops * own // seg

    def product(c, r):
        def part(index):
            span = pl.ds(pl.multiple_of(index * seg, seg), seg)
            return jnp.dot(
                adjacency[rows(r), span], gathered[c, span, :], preferred_element_type=jnp.float32
            )

        if segs == 1:
            return part(0)
        return lax.fori_loop(
            0, segs, lambda index, total: total + part(index), jnp.zeros((own, CHUNK), jnp.float32)
        )

    def part_copy(c, r, slot):
        return pltpu.make_async_remote_copy(
            src_ref=part_out.at[c, r],
            dst_ref=part_in.at[c, slot],
            send_sem=part_send.at[c, r],
            recv_sem=part_recv.at[c, slot],
            device_id={"rep": r},
            device_id_type=MESH,
        )

    def spread(c):
        def send(index):
            r = lax.rem(me + reps - 1 - index, reps)
            part_out[c, r] = product(c, r).astype(jnp.bfloat16)
            part_copy(c, r, me).start()

        repeat(reps - 1, send)
        part_in[c, me] = product(c, me).astype(jnp.bfloat16)

    scale = []

    def finish(c):
        if not scale:
            for k in range(1, reps):
                deg_arrival(lax.rem(me + k, reps)).wait_recv()
            degree = deg_in[0]
            for r in range(1, reps):
                degree += deg_in[r]
            degree = jnp.broadcast_to(degree[0:1, :] + 1.0, (CHUNK, own))
            scale.append(degree.T)
        for k in range(1, reps):
            r = lax.rem(me + k, reps)
            part_copy(c, r, r).wait_recv()
        total = gathered[c, rows(z), :].astype(jnp.float32)
        for r in range(reps):
            total += part_in[c, r].astype(jnp.float32)
        normal[:, c * CHUNK : (c + 1) * CHUNK] = (total / scale[0]).astype(jnp.bfloat16)

    for c in range(chunks):
        gather(c)
        spread(c)
        if c > 0:
            finish(c - 1)
    finish(chunks - 1)

    weight_copy.wait()
    result = jnp.dot(normal[...], weight_v[...], preferred_element_type=jnp.float32)
    out_ref[...] = jnp.maximum(result, 0.0).astype(out_ref.dtype)

    for k in range(1, reps):
        deg_copy(lax.rem(me + k, reps)).wait_send()
    for c in range(chunks):
        for k in range(1, reps):
            part_copy(c, lax.rem(me + k, reps), me).wait_send()

        def drain(source):
            @pl.when(jnp.logical_and(has_up, source <= z))
            def _():
                shift(source, c, True).wait_send()

            @pl.when(jnp.logical_and(has_down, source >= z))
            def _():
                shift(source, c, False).wait_send()

        repeat(loops, drain)


def body(features, weight, block_row, edge_row, edge_col, edge_count):
    loops = lax.axis_size("loop")
    reps = lax.axis_size("rep")
    own, width = features.shape
    chunks = width // CHUNK
    slots, edges = edge_row.shape[3:]
    listing = (loops, slots, edges)
    dma = pltpu.SemaphoreType.DMA
    return pl.pallas_call(
        functools.partial(kernel, loops, reps),
        out_shape=jax.ShapeDtypeStruct((own, weight.shape[1]), jnp.bfloat16),
        in_specs=[pl.BlockSpec(memory_space=pl.ANY)] * 6,
        out_specs=pl.BlockSpec(memory_space=pltpu.VMEM),
        scratch_shapes=[
            pltpu.VMEM((chunks, loops * own, CHUNK), jnp.bfloat16),
            pltpu.VMEM((reps * own, loops * own), jnp.bfloat16),
            pltpu.VMEM((chunks, reps, own, CHUNK), jnp.bfloat16),
            pltpu.VMEM((chunks, reps, own, CHUNK), jnp.bfloat16),
            pltpu.VMEM((reps, 8, own), jnp.float32),
            pltpu.VMEM((reps, 8, own), jnp.float32),
            pltpu.VMEM((own, width), jnp.bfloat16),
            pltpu.VMEM(weight.shape, jnp.bfloat16),
            pltpu.SMEM((loops, slots), jnp.int32),
            pltpu.VMEM(listing, jnp.int32),
            pltpu.VMEM(listing, jnp.int32),
            pltpu.VMEM(listing, jnp.int32),
            dma((5 + chunks,)),
            dma((loops, chunks)),
            dma((loops, chunks)),
            dma((loops, chunks)),
            dma((chunks, reps)),
            dma((chunks, reps)),
            dma((reps,)),
            dma((reps,)),
        ],
        compiler_params=pltpu.CompilerParams(
            collective_id=0, has_side_effects=True, vmem_limit_bytes=56 * 1024 * 1024
        ),
    )(
        features,
        weight,
        block_row.reshape(loops, slots),
        edge_row.reshape(listing),
        edge_col.reshape(listing),
        edge_count.reshape(listing),
    )


def solution(mesh):
    return jax.shard_map(
        body,
        mesh=mesh,
        in_specs=(
            P(("groups", "loop", "rep"), None),
            P(),
            P(("groups", "loop"), "rep", None, None),
            P(("groups", "loop"), "rep", None, None, None),
            P(("groups", "loop"), "rep", None, None, None),
            P(("groups", "loop"), "rep", None, None, None),
        ),
        out_specs=P(("groups", "loop", "rep"), None),
        check_vma=False,
    )
```

time: 81.8 us -> 39.3 us (0.48)
  Pallas kernels: 0 us -> 35.5 us
  other arithmetic: 28.2 us -> 0 us
  between operations: 14.2 us -> 0.01 us
  waiting for transfers between devices: 11.8 us -> 0 us
  local copies, waits for them, and re-layouts: 12.5 us -> 3.64 us
  blocking collectives: 5.67 us -> 0 us
  matrix products: 5.57 us -> 0 us
  starting transfers between devices: 3.28 us -> 0 us
    pallas_call x0 -> x1, Pallas kernels: none -> 35.5 us  [body(): pl.pallas_call(functools.partial(kernel, loops, reps), out_shape=jax.Shap...]
    scatter-add x5 -> x0, other arithmetic: 25.6 us -> none  [the longest x4 14.4 us: add_blocks(): return aggregate.at[blocks_now].add(blocks)]
    gather x4 -> x0, local copies, waits for them, and re-layouts: 8.25 us -> none  [absorb(): jnp.take(visiting, cols_now, axis=0)]
    reduce_scatter x1 -> x0, waiting for transfers between devices: 6.25 us -> none  [body(): lax.psum_scatter(aggregate.astype(jnp.bfloat16), 'rep', scatter_dimension...]
    unnamed x1 -> x0, blocking collectives: 5.67 us -> none
    dot_general x5 -> x0, matrix products: 5.57 us -> none  [the longest x4 3.57 us: add_blocks(): jnp.einsum('sbe,sef->sbf', onehot, picked, preferred_element_type=jnp.flo...]
    ppermute x3 -> x0, waiting for transfers between devices: 5.54 us -> none  [passed_along(): return lax.ppermute(value, axis, pairs)]
    ppermute x3 -> x0, starting transfers between devices: 3.28 us -> none  [passed_along(): return lax.ppermute(value, axis, pairs)]
  transfers between devices with their start and end apart: 4 -> 0, of which waited for: 4 -> 0; matrix products, arithmetic and copies ran while one was open for 40% -> 0% of each run, Pallas kernels for 0% -> 0%
where the time goes in v1:
time: 39.3 us; the launch traced here: 39.1 us
  Pallas kernels  35.5 us (90%)
  local copies, waits for them, and re-layouts  3.64 us (9%)
    pallas_call x1, Pallas kernels, body(): pl.pallas_call(functools.partial(kernel, loops, reps), out_shape=jax.Shap...  35.5 us
    unnamed x6, local copies, waits for them, and re-layouts  3.02 us

profile of v1, /device:TPU:0, one launch (start us, length us, event | category | flops | bytes accessed | tf_op | source)
XLA Modules:
  0.0 39.1 jit_solution(7810517174681690841)
XLA Ops:
  0.0 0.0 copy-start
  0.0 0.0 copy-start.1
  0.0 1.3 %copy.13 = s32[1,1,4,6,64]{4,3,2,1,0:T(8,128)} copy(s32[1,1,4,6,64]{4,2,3,1,0:T(4,128)} %param.9) | data formatting | bytes 12288 | tf_op args[3]
  1.3 0.0 copy-done
  1.3 0.0 copy-done.1
  1.3 0.6 %copy_bitcast_fusion = (s32[4,6,64]{2,1,0:T(8,128)}, s32[4,6,64]{2,1,0:T(8,128)}) fusion(s32[1,1,4,6,64]{4,2,3,1,0:T(4,128)S(1)} %copy-done, s32[1,1,4,6,64]{4,2,3,1,0:T(4,128)S(1)} %copy-done.1), kind=kLoop, calls=%fused_computation | loop fusion | bytes 24576 | tf_op jit(solution)/shard_map/reshape | solution.py:307
  2.0 35.5 %shard_map.64 = bf16[256,512]{1,0:T(8,128)(2,1)} custom-call(bf16[256,512]{1,0:T(8,128)(2,1)} %feat_hbm.1, bf16[512,512]{1,0:T(8,128)(2,1)} %weight_hbm.1, s32[4,6]{1,0:T(4,128)} %bitcast.9, s32[4,6,64]{2,1,0:T(8,128)} %bitcast.8, s32[4,6,64]{2,1,0:T(8,128)} %get-tuple-element.6.ecol_hbm, s32[4,6,64]{2,1,0:T(8,128)} %get-tuple-element.5.ecnt_hbm), custom_call_target="tpu_custom_call" | custom-call | tf_op jit(solution)/shard_map/pallas_call | solution.py:271
  37.4 1.7 %copy.15 = bf16[256,512]{1,0:T(8,128)(2,1)} copy(bf16[256,512]{1,0:T(8,128)(2,1)} %shard_map.64) | data formatting | bytes 524288
Async XLA Ops:
  0.0 1.3 %copy-start = (s32[1,1,4,6,64]{4,2,3,1,0:T(4,128)S(1)}, s32[1,1,4,6,64]{4,2,3,1,0:T(4,128)}, u32[]{:S(2)}) copy-start(s32[1,1,4,6,64]{4,2,3,1,0:T(4,128)} %param.11) | copy-start | bytes 18436
  0.0 1.3 %copy-start.1 = (s32[1,1,4,6,64]{4,2,3,1,0:T(4,128)S(1)}, s32[1,1,4,6,64]{4,2,3,1,0:T(4,128)}, u32[]{:S(2)}) copy-start(s32[1,1,4,6,64]{4,2,3,1,0:T(4,128)} %param.10) | copy-start | bytes 18436

commit v2 on v1

v2 whole, which is shorter than its diff:
```python
import functools

import jax
import jax.numpy as jnp
from jax import lax
from jax.experimental import pallas as pl
from jax.experimental.pallas import tpu as pltpu
from jax.sharding import PartitionSpec as P

BLOCK = 128
CHUNK = 128
MESH = pl.DeviceIdType.MESH
NT = (((1,), (1,)), ((), ()))


def repeat(count, step, most=4):
    if count <= most:
        for index in range(count):
            step(index)
    else:
        lax.fori_loop(0, count, lambda index, carry: (step(index), carry)[1], 0)


def when(condition, step):
    if condition is True:
        step()
    elif condition is not False:
        pl.when(condition)(step)


def kernel(
    loops, reps, helped,
    feat_hbm, brow_hbm, erow_hbm, ecol_hbm, ecnt_hbm,
    out_ref,
    gathered, adjacency, mine, sib_out, sib_in, chip_out, chip_in, kept, end_out, end_in,
    deg_out, deg_in, scale, brow_v, lists, end_lists,
    local_sem, up_send, down_send, gather_recv, sib_send, sib_recv, chip_send, chip_recv,
    end_send, end_recv, list_send, list_recv, deg_send, deg_recv,
):
    own, width = feat_hbm.shape
    chunks = width // CHUNK
    slots, _, edges = erow_hbm.shape
    cores = 2 if reps % 2 == 0 else 1
    chips = reps // cores
    z = lax.axis_index("loop")
    me = lax.axis_index("rep")
    chip = lax.div(me, cores)
    core = lax.rem(me, cores)
    has_up = z < loops - 1
    has_down = z > 0
    inner = jnp.logical_and(has_up, has_down)
    at_end = jnp.logical_not(inner)
    helps_low = z == 1
    helps = jnp.logical_or(helps_low, z == loops - 2)
    end_z = jnp.where(helps_low, 0, loops - 1)
    helper_z = jnp.where(has_down, loops - 2, 1)

    def rows(index):
        return pl.ds(pl.multiple_of(index * own, own), own)

    small = [
        pltpu.make_async_copy(brow_hbm, brow_v, local_sem.at[0]),
        pltpu.make_async_copy(erow_hbm, lists.at[0], local_sem.at[1]),
        pltpu.make_async_copy(ecol_hbm, lists.at[1], local_sem.at[2]),
        pltpu.make_async_copy(ecnt_hbm, lists.at[2], local_sem.at[3]),
    ]
    own_copy = [
        pltpu.make_async_copy(
            feat_hbm.at[:, pl.ds(c * CHUNK, CHUNK)], gathered.at[c, rows(z)], local_sem.at[4 + c]
        )
        for c in range(chunks)
    ]
    for copy in own_copy + small:
        copy.start()

    barrier = pltpu.get_barrier_semaphore()

    @pl.when(has_up)
    def _():
        pl.semaphore_signal(barrier, inc=1, device_id={"loop": z + 1}, device_id_type=MESH)

    @pl.when(has_down)
    def _():
        pl.semaphore_signal(barrier, inc=1, device_id={"loop": z - 1}, device_id_type=MESH)

    for k in range(1, reps):
        pl.semaphore_signal(
            barrier, inc=1, device_id={"rep": lax.rem(me + k, reps)}, device_id_type=MESH
        )

    for copy in small:
        copy.wait()
    for s in range(slots):
        lists[0, s] = lists[0, s] + brow_v[:, s : s + 1] * BLOCK
    for c in range(chunks):
        own_copy[c].wait()
    pl.semaphore_wait(barrier, reps - 1 + has_up.astype(jnp.int32) + has_down.astype(jnp.int32))

    def shift(source, c, up):
        return pltpu.make_async_remote_copy(
            src_ref=gathered.at[c, rows(source)],
            dst_ref=gathered.at[c, rows(source)],
            send_sem=(up_send if up else down_send).at[source, c],
            recv_sem=gather_recv.at[source, c],
            device_id={"loop": z + 1 if up else z - 1},
            device_id_type=MESH,
        )

    def sends(c, up):
        if c < helped:
            return z + 1 < loops - 1 if up else z - 1 > 0
        return has_up if up else has_down

    def takes(c):
        return inner if c < helped else True

    def send_own(c, up, condition):
        when(jnp.logical_and(sends(c, up), condition), lambda: shift(z, c, up).start())

    ahead = 2

    def early(up):
        if not helped:
            return z == (0 if up else loops - 1)
        return jnp.logical_or(at_end, z + 1 == loops - 1 if up else z - 1 == 0)

    for c in range(chunks):
        for up in (True, False):
            send_own(c, up, c < ahead or early(up))

    def list_copy(kind, to):
        return pltpu.make_async_remote_copy(
            src_ref=lists.at[kind],
            dst_ref=end_lists.at[kind],
            send_sem=list_send.at[kind],
            recv_sem=list_recv.at[kind],
            device_id={"loop": to},
            device_id_type=MESH,
        )

    if helped:

        @pl.when(at_end)
        def _():
            for kind in range(3):
                list_copy(kind, helper_z).start()

    listed = slots * edges
    position = lax.broadcasted_iota(jnp.int32, (own, listed), 0)
    ones = jnp.ones((8, listed), jnp.bfloat16)
    deg_out[...] = jnp.zeros_like(deg_out)

    def build(held, which, source):
        def joined(kind):
            return jnp.concatenate(
                [held[kind, s, pl.ds(source, 1), :] for s in range(slots)], axis=1
            )

        target = joined(0)
        column = joined(1)
        count = joined(2).astype(jnp.float32)
        pick = jnp.where(position == column, 1.0, 0.0).astype(jnp.bfloat16)

        def build_rows(r):
            place = jnp.where(position == target - r * own, count, 0.0).astype(jnp.bfloat16)
            block = lax.dot_general(place, pick, NT, preferred_element_type=jnp.float32)
            adjacency[which, rows(r), rows(source)] = block.astype(jnp.bfloat16)
            if which == 0:
                deg_out[r] += lax.dot_general(ones, place, NT, preferred_element_type=jnp.float32)

        repeat(reps, build_rows)

    repeat(loops, lambda source: build(lists, 0, source))

    def deg_copy(r, slot):
        return pltpu.make_async_remote_copy(
            src_ref=deg_out.at[r],
            dst_ref=deg_in.at[slot],
            send_sem=deg_send.at[r],
            recv_sem=deg_recv.at[slot],
            device_id={"rep": r},
            device_id_type=MESH,
        )

    deg_out[...] = deg_out[...].astype(jnp.bfloat16).astype(jnp.float32)
    deg_in[me] = deg_out[me]
    for k in range(1, reps):
        deg_copy(lax.rem(me + k, reps), me).start()

    if helped:

        @pl.when(helps)
        def _():
            for kind in range(3):
                list_copy(kind, end_z).wait_recv()
            repeat(loops, lambda source: build(end_lists, 1, source))

    def gather(c):
        def hop(index):
            below = z - 1 - index
            above = z + 1 + index

            @pl.when(below >= 0)
            def _():
                shift(below, c, True).wait_recv()
                when(sends(c, True), lambda: shift(below, c, True).start())

            @pl.when(above < loops)
            def _():
                shift(above, c, False).wait_recv()
                when(sends(c, False), lambda: shift(above, c, False).start())

        repeat(loops - 1, hop)

    seg = min(loops, 4) * own
    segs = loops * own // seg

    def product(which, c, r):
        def part(index):
            span = pl.ds(pl.multiple_of(index * seg, seg), seg)
            return jnp.dot(
                adjacency[which, rows(r), span],
                gathered[c, span, :],
                preferred_element_type=jnp.float32,
            )

        if segs == 1:
            return part(0)
        return lax.fori_loop(
            0, segs, lambda index, total: total + part(index), jnp.zeros((own, CHUNK), jnp.float32)
        )

    def sib_copy(job):
        return pltpu.make_async_remote_copy(
            src_ref=sib_out.at[job],
            dst_ref=sib_in.at[job],
            send_sem=sib_send.at[job],
            recv_sem=sib_recv.at[job],
            device_id={"rep": chip * cores + 1 - core},
            device_id_type=MESH,
        )

    def chip_copy(job, other, slot):
        return pltpu.make_async_remote_copy(
            src_ref=chip_out.at[job, other],
            dst_ref=chip_in.at[job, slot],
            send_sem=chip_send.at[job, other],
            recv_sem=chip_recv.at[job, slot],
            device_id={"rep": other * cores + core},
            device_id_type=MESH,
        )

    def end_copy(c, to):
        return pltpu.make_async_remote_copy(
            src_ref=end_out.at[c],
            dst_ref=end_in.at[c],
            send_sem=end_send.at[c],
            recv_sem=end_recv.at[c],
            device_id={"loop": to},
            device_id_type=MESH,
        )

    def multiply(which, c):
        job = which * chunks + c

        if cores == 2:

            def theirs(x):
                value = product(which, c, x * cores + 1 - core)
                sib_out[job, x] = value.astype(jnp.bfloat16)

            repeat(chips, theirs)
            sib_copy(job).start()

        def ours(x):
            mine[which, x] = product(which, c, x * cores + core)

        repeat(chips, ours)

    def cross(which, c):
        job = which * chunks + c
        if cores == 2:
            sib_copy(job).wait_recv()

        def summed(x):
            total = mine[which, x]
            if cores == 2:
                total += sib_in[job, x].astype(jnp.float32)
            return total

        def send(index):
            other = lax.rem(chip + 1 + index, chips)
            chip_out[job, other] = summed(other).astype(jnp.bfloat16)
            chip_copy(job, other, chip).start()

        repeat(chips - 1, send)
        kept[job] = summed(chip)

    def received(which, c):
        job = which * chunks + c
        total = kept[job]
        for k in range(1, chips):
            other = lax.rem(chip + k, chips)
            chip_copy(job, other, other).wait_recv()
            total += chip_in[job, other].astype(jnp.float32)
        return total

    def put(c, total):
        total += gathered[c, rows(z), :].astype(jnp.float32)
        out_ref[:, c * CHUNK : (c + 1) * CHUNK] = (total / scale[...]).astype(jnp.bfloat16)

    def start_job(c):
        if c < helped:
            pl.when(helps)(lambda: multiply(1, c))
        multiply(0, c)
        if c < helped:
            pl.when(helps)(lambda: cross(1, c))
        cross(0, c)

    def end_job(c):
        if c < helped:

            @pl.when(helps)
            def _():
                end_out[c] = received(1, c).astype(jnp.bfloat16)
                end_copy(c, end_z).start()

        put(c, received(0, c))

    def degrees():
        for k in range(1, reps):
            r = lax.rem(me + k, reps)
            deg_copy(r, r).wait_recv()
        degree = deg_in[0]
        for r in range(1, reps):
            degree += deg_in[r]
        scale[...] = jnp.broadcast_to(degree[0:1, :] + 1.0, (CHUNK, own)).T

    for c in range(chunks):

        def step(c=c):
            gather(c)
            if c + ahead < chunks:
                for up in (True, False):
                    send_own(c + ahead, up, jnp.logical_not(early(up)))
            start_job(c)

        when(takes(c), step)
        if c == 0:
            degrees()
        if c > 0:
            when(takes(c - 1), lambda: end_job(c - 1))
    if helped:

        @pl.when(at_end)
        def _():
            for c in range(helped):
                end_copy(c, helper_z).wait_recv()
                put(c, end_in[c].astype(jnp.float32))

    end_job(chunks - 1)

    for k in range(1, reps):
        deg_copy(lax.rem(me + k, reps), me).wait_send()
    if helped:

        @pl.when(at_end)
        def _():
            for kind in range(3):
                list_copy(kind, helper_z).wait_send()

    def job_left(job):
        if cores == 2:
            sib_copy(job).wait_send()
        for k in range(1, chips):
            chip_copy(job, lax.rem(chip + k, chips), chip).wait_send()

    for c in range(chunks):
        when(takes(c), lambda: job_left(c))
        if c < helped:

            @pl.when(helps)
            def _():
                job_left(chunks + c)
                end_copy(c, end_z).wait_send()

        def drain(source):
            when(
                jnp.logical_and(sends(c, True), source <= z),
                lambda: shift(source, c, True).wait_send(),
            )
            when(
                jnp.logical_and(sends(c, False), source >= z),
                lambda: shift(source, c, False).wait_send(),
            )

        repeat(loops, drain)


def body(features, weight, block_row, edge_row, edge_col, edge_count):
    loops = lax.axis_size("loop")
    reps = lax.axis_size("rep")
    own, width = features.shape
    chunks = width // CHUNK
    slots, edges = edge_row.shape[3:]
    chips = reps // 2 if reps % 2 == 0 else reps
    adjacency_bytes = reps * own * loops * own * 2
    helped = chunks // 2 if loops >= 4 and adjacency_bytes <= 8 * 1024 * 1024 else 0
    kinds = 2 if helped else 1
    jobs = chunks + helped
    listing = (slots, loops, edges)
    dma = pltpu.SemaphoreType.DMA
    bf16, f32, i32 = jnp.bfloat16, jnp.float32, jnp.int32

    def stored(array):
        return jnp.swapaxes(array.reshape(loops, slots, edges), 0, 1)

    normalized = pl.pallas_call(
        functools.partial(kernel, loops, reps, helped),
        out_shape=jax.ShapeDtypeStruct((own, width), bf16),
        in_specs=[pl.BlockSpec(memory_space=pl.ANY)] * 5,
        out_specs=pl.BlockSpec(memory_space=pltpu.VMEM),
        scratch_shapes=[
            pltpu.VMEM((chunks, loops * own, CHUNK), bf16),
            pltpu.VMEM((kinds, reps * own, loops * own), bf16),
            pltpu.VMEM((kinds, chips, own, CHUNK), f32),
            pltpu.VMEM((jobs, chips, own, CHUNK), bf16),
            pltpu.VMEM((jobs, chips, own, CHUNK), bf16),
            pltpu.VMEM((jobs, chips, own, CHUNK), bf16),
            pltpu.VMEM((jobs, chips, own, CHUNK), bf16),
            pltpu.VMEM((jobs, own, CHUNK), f32),
            pltpu.VMEM((max(helped, 1), own, CHUNK), bf16),
            pltpu.VMEM((max(helped, 1), own, CHUNK), bf16),
            pltpu.VMEM((reps, 8, own), f32),
            pltpu.VMEM((reps, 8, own), f32),
            pltpu.VMEM((own, CHUNK), f32),
            pltpu.VMEM((loops, slots), i32),
            pltpu.VMEM((3,) + listing, i32),
            pltpu.VMEM((3,) + listing, i32),
            dma((4 + chunks,)),
            dma((loops, chunks)),
            dma((loops, chunks)),
            dma((loops, chunks)),
            dma((jobs,)),
            dma((jobs,)),
            dma((jobs, chips)),
            dma((jobs, chips)),
            dma((max(helped, 1),)),
            dma((max(helped, 1),)),
            dma((3,)),
            dma((3,)),
            dma((reps,)),
            dma((reps,)),
        ],
        compiler_params=pltpu.CompilerParams(
            collective_id=0, has_side_effects=True, vmem_limit_bytes=56 * 1024 * 1024
        ),
    )(
        features,
        block_row.reshape(loops, slots),
        stored(edge_row),
        stored(edge_col),
        stored(edge_count),
    )
    product = jnp.dot(normalized, weight, preferred_element_type=f32)
    return jnp.maximum(product, 0.0).astype(bf16)


def solution(mesh):
    return jax.shard_map(
        body,
        mesh=mesh,
        in_specs=(
            P(("groups", "loop", "rep"), None),
            P(),
            P(("groups", "loop"), "rep", None, None),
            P(("groups", "loop"), "rep", None, None, None),
            P(("groups", "loop"), "rep", None, None, None),
            P(("groups", "loop"), "rep", None, None, None),
        ),
        out_specs=P(("groups", "loop", "rep"), None),
        check_vma=False,
    )
```

time: 39.3 us -> 45.5 us (1.16)
  Pallas kernels: 35.5 us -> 43.3 us
  local copies, waits for them, and re-layouts: 3.64 us -> 0.01 us
  matrix products: 0 us -> 1.96 us
    pallas_call x1, Pallas kernels: 35.5 us -> 43.3 us  [body(): pl.pallas_call(functools.partial(kernel, loops, reps, helped), out_shape=...]
    unnamed x6 -> x2, local copies, waits for them, and re-layouts: 3.02 us -> 0.01 us
    dot_general x0 -> x1, matrix products: none -> 1.96 us  [body(): product = jnp.dot(normalized, weight, preferred_element_type=f32)]
    reshape x1 -> x0, local copies, waits for them, and re-layouts: 0.62 us -> none  [body(): edge_count.reshape(listing)]
where the time goes in v2:
time: 45.5 us; the launch traced here: 45.3 us
  Pallas kernels  43.3 us (95%)
  matrix products  1.96 us (4%)
    pallas_call x1, Pallas kernels, body(): pl.pallas_call(functools.partial(kernel, loops, reps, helped), out_shape=...  43.3 us
    dot_general x1, matrix products, body(): product = jnp.dot(normalized, weight, preferred_element_type=f32)  1.96 us

profile of v2, /device:TPU:0, one launch (start us, length us, event | category | flops | bytes accessed | tf_op | source)
XLA Modules:
  0.0 45.3 jit_solution(6944334967097430635)
XLA Ops:
  0.0 0.0 copy-start
  0.0 43.3 %shard_map.64 = bf16[256,512]{1,0:T(8,128)(2,1)} custom-call(bf16[256,512]{1,0:T(8,128)(2,1)} %feat_hbm.1, s32[4,6]{1,0:T(4,128)} %bitcast.15, s32[6,4,64]{2,1,0:T(4,128)} %bitcast.12, s32[6,4,64]{2,1,0:T(4,128)} %bitcast.13, s32[6,4,64]{2,1,0:T(4,128)} %bitcast.14), custom_call_target="tpu_custom_call" | custom-call | tf_op jit(solution)/shard_map/pallas_call | solution.py:418
  43.3 0.0 copy-done
  43.3 2.0 %fusion = bf16[256,512]{1,0:T(8,128)(2,1)} fusion(bf16[256,512]{1,0:T(8,128)(2,1)} %shard_map.64, bf16[512,512]{1,0:T(8,128)(2,1)S(1)} %copy-done), kind=kOutput, calls=%fused_computation.1 | convolution fusion | flops 134479872 | bytes 1048576 | tf_op jit(solution)/shard_map/dot_general | solution.py:465
Async XLA Ops:
  0.0 43.3 %copy-start = (bf16[512,512]{1,0:T(8,128)(2,1)S(1)}, bf16[512,512]{1,0:T(8,128)(2,1)}, u32[]{:S(2)}) copy-start(bf16[512,512]{1,0:T(8,128)(2,1)} %param.7) | copy-start | bytes 1572868

commit v3 on v2

--- a/solution.py
+++ b/solution.py
@@ -8,7 +8,7 @@
 from jax.sharding import PartitionSpec as P
 
 BLOCK = 128
-CHUNK = 128
+CHUNK = 256
 MESH = pl.DeviceIdType.MESH
 NT = (((1,), (1,)), ((), ()))
 
@@ -114,20 +114,6 @@
     def takes(c):
         return inner if c < helped else True
 
-    def send_own(c, up, condition):
-        when(jnp.logical_and(sends(c, up), condition), lambda: shift(z, c, up).start())
-
-    ahead = 2
-
-    def early(up):
-        if not helped:
-            return z == (0 if up else loops - 1)
-        return jnp.logical_or(at_end, z + 1 == loops - 1 if up else z - 1 == 0)
-
-    for c in range(chunks):
-        for up in (True, False):
-            send_own(c, up, c < ahead or early(up))
-
     def list_copy(kind, to):
         return pltpu.make_async_remote_copy(
             src_ref=lists.at[kind],
@@ -144,6 +130,10 @@
         def _():
             for kind in range(3):
                 list_copy(kind, helper_z).start()
+
+    for c in range(chunks):
+        for up in (True, False):
+            when(sends(c, up), lambda: shift(z, c, up).start())
 
     listed = slots * edges
     position = lax.broadcasted_iota(jnp.int32, (own, listed), 0)
@@ -195,22 +185,25 @@
                 list_copy(kind, end_z).wait_recv()
             repeat(loops, lambda source: build(end_lists, 1, source))
 
+    def hop(c, index):
+        below = z - 1 - index
+        above = z + 1 + index
+
+        @pl.when(below >= 0)
+        def _():
+            shift(below, c, True).wait_recv()
+            when(sends(c, True), lambda: shift(below, c, True).start())
+
+        @pl.when(above < loops)
+        def _():
+            shift(above, c, False).wait_recv()
+            when(sends(c, False), lambda: shift(above, c, False).start())
+
+    for c in range(chunks):
+        when(takes(c), lambda: hop(c, 0))
+
     def gather(c):
-        def hop(index):
-            below = z - 1 - index
-            above = z + 1 + index
-
-            @pl.when(below >= 0)
-            def _():
-                shift(below, c, True).wait_recv()
-                when(sends(c, True), lambda: shift(below, c, True).start())
-
-            @pl.when(above < loops)
-            def _():
-                shift(above, c, False).wait_recv()
-                when(sends(c, False), lambda: shift(above, c, False).start())
-
-        repeat(loops - 1, hop)
+        repeat(loops - 2, lambda index: hop(c, index + 1))
 
     seg = min(loops, 4) * own
     segs = loops * own // seg
@@ -340,9 +333,6 @@
 
         def step(c=c):
             gather(c)
-            if c + ahead < chunks:
-                for up in (True, False):
-                    send_own(c + ahead, up, jnp.logical_not(early(up)))
             start_job(c)
 
         when(takes(c), step)
@@ -404,8 +394,7 @@
     chunks = width // CHUNK
     slots, edges = edge_row.shape[3:]
     chips = reps // 2 if reps % 2 == 0 else reps
-    adjacency_bytes = reps * own * loops * own * 2
-    helped = chunks // 2 if loops >= 4 and adjacency_bytes <= 8 * 1024 * 1024 else 0
+    helped = 0
     kinds = 2 if helped else 1
     jobs = chunks + helped
     listing = (slots, loops, edges)

time: 45.5 us -> 32.6 us (0.72)
  Pallas kernels: 43.3 us -> 30.4 us
    pallas_call x1, Pallas kernels: 43.3 us -> 30.4 us  [body(): pl.pallas_call(functools.partial(kernel, loops, reps, helped), out_shape=...]
where the time goes in v3:
time: 32.6 us; the launch traced here: 32.4 us
  Pallas kernels  30.4 us (93%)
  matrix products  1.96 us (6%)
    pallas_call x1, Pallas kernels, body(): pl.pallas_call(functools.partial(kernel, loops, reps, helped), out_shape=...  30.4 us
    dot_general x1, matrix products, body(): product = jnp.dot(normalized, weight, preferred_element_type=f32)  1.96 us

profile of v3, /device:TPU:0, one launch (start us, length us, event | category | flops | bytes accessed | tf_op | source)
XLA Modules:
  0.0 32.4 jit_solution(11971191025323237778)
XLA Ops:
  0.0 0.0 copy-start
  0.0 30.4 %shard_map.64 = bf16[256,512]{1,0:T(8,128)(2,1)} custom-call(bf16[256,512]{1,0:T(8,128)(2,1)} %feat_hbm.1, s32[4,6]{1,0:T(4,128)} %bitcast.15, s32[6,4,64]{2,1,0:T(4,128)} %bitcast.12, s32[6,4,64]{2,1,0:T(4,128)} %bitcast.13, s32[6,4,64]{2,1,0:T(4,128)} %bitcast.14), custom_call_target="tpu_custom_call" | custom-call | tf_op jit(solution)/shard_map/pallas_call | solution.py:407
  30.4 0.0 copy-done
  30.4 2.0 %fusion = bf16[256,512]{1,0:T(8,128)(2,1)} fusion(bf16[256,512]{1,0:T(8,128)(2,1)} %shard_map.64, bf16[512,512]{1,0:T(8,128)(2,1)S(1)} %copy-done), kind=kOutput, calls=%fused_computation.1 | convolution fusion | flops 134479872 | bytes 1048576 | tf_op jit(solution)/shard_map/dot_general | solution.py:454
Async XLA Ops:
  0.0 30.4 %copy-start = (bf16[512,512]{1,0:T(8,128)(2,1)S(1)}, bf16[512,512]{1,0:T(8,128)(2,1)}, u32[]{:S(2)}) copy-start(bf16[512,512]{1,0:T(8,128)(2,1)} %param.7) | copy-start | bytes 1572868
